TPU v7x, 512 devices: a whole 4x4x16 slice. The times are simulated.
512 devices in a mesh: frame: 32 (over y_lo, z), slab: 16 (over x, y_hi, core).
Axes of the slice: x: 4, y: 4 (y_hi: 2, y_lo: 2; y = y_hi * 2 + y_lo), z: 16, core: 2. Of those that a mesh axis runs over, the one named last changes fastest.
Arguments:
- pano: bfloat16 [512, 256, 320], P('frame', 'slab'), parts along dimension 0, may hold values from -6 to 6
- views: bfloat16 [1024, 16, 16, 320], P(('frame', 'slab')), parts along dimension 0, may hold values from -6 to 6
- view_count: int32 [512], P('frame'), parts along dimension 0, may hold values from 0 to 2, as said below
- links: int32 [1024, 2], P('frame'), parts along dimension 0, may hold values from 0 to 2
- pano_conv1: bfloat16 [9, 320, 320], P(None, 'slab'), may hold values from -0.109375 to 0.109375
- pano_conv2: bfloat16 [9, 320, 320], P(None, 'slab'), may hold values from -0.109375 to 0.109375
- view_conv1: bfloat16 [9, 320, 320], P(None, 'slab'), may hold values from -0.109375 to 0.109375
- view_conv2: bfloat16 [9, 320, 320], P(None, 'slab'), may hold values from -0.109375 to 0.109375
- p2v_query: bfloat16 [320, 320], replicated, may hold values from -0.6 to 0.6
- p2v_key: bfloat16 [320, 320], replicated, may hold values from -0.6 to 0.6
- p2v_value: bfloat16 [320, 320], replicated, may hold values from -0.3125 to 0.3125
- p2v_out: bfloat16 [320, 320], replicated, may hold values from -0.3125 to 0.3125
- v2p_query: bfloat16 [320, 320], replicated, may hold values from -0.6 to 0.6
- v2p_key: bfloat16 [320, 320], replicated, may hold values from -0.6 to 0.6
- v2p_value: bfloat16 [320, 320], replicated, may hold values from -0.3125 to 0.3125
- v2p_out: bfloat16 [320, 320], replicated, may hold values from -0.3125 to 0.3125
Outputs:
- pano_out: bfloat16 [512, 256, 320], P('frame', 'slab'), parts along dimension 0
- view_out: bfloat16 [1024, 16, 16, 320], P(('frame', 'slab')), parts along dimension 0
There are 32 independent parts, one for each index of `frame`. A program takes and returns all parts, laid end to end along the dimension named above; an argument that names none is the same for every part. Nothing has to cross between parts.
Inputs may be any that keep to these rules, and one draw needn't show every extreme that they name: `view_count`: in every frame some slab has no occupied slot and some has 2.
All inputs are finite; a program needn't handle non-finite values.
Results may differ from a plain program's by a relative error of at most 0.0085.
Values may be sent and summed in bfloat16 or wider, within the bound.
A program may use at most 64 MiB of HBM per device.

v0:
```python
import jax
import jax.numpy as jnp
from jax import lax
from jax.sharding import PartitionSpec as P

HEADS = 5


def padded_2(cells, sides, width):
    for axis, dim in sides:
        count = lax.axis_size(axis)
        head = lax.slice_in_dim(cells, 0, width, axis=dim)
        tail = lax.slice_in_dim(cells, cells.shape[dim] - width, cells.shape[dim], axis=dim)
        cells = jnp.concatenate(
            [
                lax.ppermute(tail, axis, [(i, (i + 1) % count) for i in range(count)]),
                cells,
                lax.ppermute(head, axis, [((i + 1) % count, i) for i in range(count)]),
            ],
            axis=dim,
        )
    return cells


def joined_along(blocks, dim):
    blocks = jnp.moveaxis(blocks, 0, dim)
    shape = blocks.shape
    return blocks.reshape(*shape[:dim], shape[dim] * shape[dim + 1], *shape[dim + 2 :])


def sent_to_all(array, axis):
    devices = lax.axis_size(axis)
    return lax.all_to_all(
        jnp.broadcast_to(array[None], (devices, *array.shape)), axis, 0, 0, tiled=True
    )


def gather_directly(array, axis, dim):
    return joined_along(sent_to_all(array, axis), dim)


def sent_together(arrays, axis, dim, along):
    widths = [a.shape[along] for a in arrays]
    both = jnp.concatenate(arrays, axis=along)
    filled = lax.all_gather(both, axis, axis=dim, tiled=True)
    return tuple(jnp.split(filled, [sum(widths[:k]) for k in range(1, len(widths))], axis=along))


def tap_stack(padded, lat_rows, lon_cols):
    shifted = [
        padded[:, row_step : row_step + lat_rows, col_step : col_step + lon_cols, :]
        for row_step in range(3)
        for col_step in range(3)
    ]
    return jnp.stack(shifted, axis=3).reshape(-1, 9, padded.shape[-1])


def band_pad(feature):
    return jnp.pad(feature, ((1, 1), (0, 0), (0, 0)))[None]


def fold_taps(columns, weight_rows):
    return jnp.einsum("tkc,kcd->td", columns, weight_rows, preferred_element_type=jnp.float32)


def view_conv(feature, weight):
    padded = jnp.pad(feature, ((1, 1), (1, 1), (0, 0)))[None]
    columns = tap_stack(padded, feature.shape[0], feature.shape[1])
    result = jnp.einsum("tkc,kcd->td", columns, weight, preferred_element_type=jnp.float32)
    return result.reshape(feature.shape[0], feature.shape[1], weight.shape[2])


def project(feature, weight):
    return jnp.dot(feature, weight, preferred_element_type=jnp.float32).astype(jnp.bfloat16)


def body(
    pano,
    views,
    view_count,
    links,
    pano_conv1,
    pano_conv2,
    view_conv1,
    view_conv2,
    p2v_query,
    p2v_key,
    p2v_value,
    p2v_out,
    v2p_query,
    v2p_key,
    v2p_value,
    v2p_out,
):
    lat_rows, slab_cols, channels = pano.shape
    slot_count = views.shape[0]
    view_tokens = views.shape[1] * views.shape[2]
    band_count = lat_rows // slab_cols
    head_width = channels // HEADS
    scaling = head_width ** (-0.5)
    slab_total = lax.axis_size("slab")
    position = lax.axis_index("slab")
    edged = padded_2(pano, (("slab", 1),), 2)
    inner_cols = edged.shape[1] - 2
    columns = tap_stack(band_pad(edged), lat_rows, inner_cols)
    first = fold_taps(columns, gather_directly(pano_conv1, "slab", 1))
    hidden = jax.nn.silu(first).astype(jnp.bfloat16).reshape(lat_rows, inner_cols, channels)
    columns_two = tap_stack(band_pad(hidden), lat_rows, slab_cols)
    second = fold_taps(columns_two, gather_directly(pano_conv2, "slab", 1))
    pano_mid = pano.astype(jnp.float32).reshape(lat_rows * slab_cols, channels) + second
    full_one, full_two = sent_together((view_conv1, view_conv2), "slab", 1, 0)

    def view_branch(feature):
        inner = jax.nn.silu(view_conv(feature, full_one)).astype(jnp.bfloat16)
        return feature.astype(jnp.float32) + view_conv(inner, full_two)

    def vacant(feature):
        return jnp.zeros(feature.shape, jnp.float32)

    def count_at(shift_by):
        return lax.dynamic_index_in_dim(
            view_count, (position + shift_by) % slab_total, 0, keepdims=False
        )

    own_count = count_at(0)
    outcome = [
        lax.cond(slot_index < own_count, view_branch, vacant, views[slot_index])
        for slot_index in range(slot_count)
    ]
    view_mid = jnp.stack(outcome).reshape(slot_count * view_tokens, channels)
    pano_feat = pano_mid.astype(jnp.bfloat16)
    view_feat = view_mid.astype(jnp.bfloat16)
    pano_pair_weight = jnp.concatenate([v2p_key, v2p_value], axis=1)
    view_pair_weight = jnp.concatenate([p2v_key, p2v_value], axis=1)
    nearby_pano = padded_2(pano_feat[None], (("slab", 0),), 1)
    pano_pairs = project(nearby_pano.reshape(-1, channels), pano_pair_weight)
    nearby_view = padded_2(
        view_feat.reshape(slot_count, view_tokens, channels), (("slab", 0),), slot_count
    )
    view_pairs = project(nearby_view.reshape(-1, channels), view_pair_weight)
    pano_blocks = pano_pairs.reshape(3 * band_count, view_tokens, 2 * channels)
    group_count = 3 * slot_count
    view_rows = view_pairs.reshape(group_count, view_tokens, 2 * channels)
    view_query = project(view_feat, v2p_query).reshape(slot_count, view_tokens, HEADS, head_width)
    own_links = lax.dynamic_slice_in_dim(links, position * slot_count, slot_count, 0)
    chosen = pano_blocks[own_links].reshape(slot_count, -1, 2 * channels)
    key_rows = chosen[:, :, :channels].reshape(slot_count, -1, HEADS, head_width)
    value_rows = chosen[:, :, channels:].reshape(slot_count, -1, HEADS, head_width)
    scores = (
        jnp.einsum("sqhd,skhd->shqk", view_query, key_rows, preferred_element_type=jnp.float32)
        * scaling
    )
    highest = jnp.max(scores, axis=-1, keepdims=True)
    weights = jnp.exp(scores - highest)
    shares = (weights / jnp.sum(weights, axis=-1, keepdims=True)).astype(jnp.bfloat16)
    attended = jnp.einsum(
        "shqk,skhd->sqhd", shares, value_rows, preferred_element_type=jnp.float32
    ).astype(jnp.bfloat16)
    view_delta = jnp.dot(
        attended.reshape(-1, channels), v2p_out, preferred_element_type=jnp.float32
    )
    occupied = jnp.arange(slot_count) < own_count
    view_total = (view_mid + view_delta).reshape(slot_count, view_tokens, channels)
    view_out = (
        jnp.where(occupied[:, None, None], view_total, 0.0)
        .astype(jnp.bfloat16)
        .reshape(views.shape)
    )
    pano_query = project(pano_feat, p2v_query).reshape(band_count, view_tokens, HEADS, head_width)
    near_links = jnp.stack(
        [
            lax.dynamic_slice_in_dim(
                links, (position + offset) % slab_total * slot_count, slot_count, 0
            )
            for offset in (-1, 0, 1)
        ]
    )
    near_counts = jnp.stack([count_at(offset) for offset in (-1, 0, 1)])
    wanted = (2 - jnp.arange(3))[:, None, None, None] * band_count + jnp.arange(band_count)[
        None, None, None, :
    ]
    linked = jnp.any(near_links[..., None] == wanted, axis=2)
    present = jnp.arange(slot_count)[None, :] < near_counts[:, None]
    allowed = (linked & present[..., None]).transpose(2, 0, 1).reshape(band_count, group_count)
    group_mask = allowed[:, None, None, :]
    near_keys = view_rows[:, :, :channels].reshape(group_count, view_tokens, HEADS, head_width)
    near_values = view_rows[:, :, channels:].reshape(group_count, view_tokens, HEADS, head_width)
    scores_two = (
        jnp.einsum("rqhd,gkhd->rhqgk", pano_query, near_keys, preferred_element_type=jnp.float32)
        * scaling
    )
    group_top = jnp.where(group_mask, jnp.max(scores_two, axis=-1), -jnp.inf)
    highest_two = jnp.maximum(jnp.max(group_top, axis=-1), 0.0)[..., None, None]
    weights_two = jnp.where(group_mask[..., None], jnp.exp(scores_two - highest_two), 0.0)
    total_two = jnp.sum(weights_two, axis=(-2, -1), keepdims=True) + jnp.exp(-highest_two)
    shares_two = (weights_two / total_two).astype(jnp.bfloat16)
    attended_two = jnp.einsum(
        "rhqgk,gkhd->rqhd", shares_two, near_values, preferred_element_type=jnp.float32
    ).astype(jnp.bfloat16)
    pano_delta = jnp.dot(
        attended_two.reshape(-1, channels), p2v_out, preferred_element_type=jnp.float32
    )
    pano_out = (pano_mid + pano_delta).astype(jnp.bfloat16).reshape(pano.shape)
    return (pano_out, view_out)


def solution(mesh):
    in_specs = (
        P("frame", "slab", None),
        P(("frame", "slab"), None, None, None),
        P("frame"),
        P("frame", None),
        P(None, "slab", None),
        P(None, "slab", None),
        P(None, "slab", None),
        P(None, "slab", None),
        P(),
        P(),
        P(),
        P(),
        P(),
        P(),
        P(),
        P(),
    )
    out_specs = (P("frame", "slab", None), P(("frame", "slab"), None, None, None))
    return jax.shard_map(body, mesh=mesh, in_specs=in_specs, out_specs=out_specs, check_vma=False)
```

profile of v0, /device:TPU:497, one launch (start us, length us, event | category | flops | bytes accessed | tf_op | source)
XLA Modules:
  0.0 213.2 jit_solution(4754792867055968497)
XLA Ops:
  11.9 7.7 %all-to-all-start = ((bf16[16,9,20,320]{3,2,1,0:T(8,128)(2,1)}), bf16[16,9,20,320]{3,2,1,0:T(8,128)(2,1)S(1)}, u32[]{:S(2)}, u32[]{:S(2)}) async-start(bf16[16,9,20,320]{3,2,1,0:T(8,128)(2,1)} %broadcast_in_dim.83), calls=%async_computation | async-start | bytes 5308416 | tf_op jit(solution)/shard_map/all_to_all | solution.py:33
  20.3 2.3 %collective-permute-start.1 = (bf16[16,2,320]{2,1,0:T(2,128)(2,1)}, bf16[16,2,320]{2,1,0:T(2,128)(2,1)S(1)}, u32[]{:S(2)}, u32[]{:S(2)}) collective-permute-start(bf16[16,2,320]{2,1,0:T(2,128)(2,1)} %get-tuple-element.99), channel_id=1, source_target_pairs={{1,0},{2,1},{3,2},{4,3},{5,4},{6,5},{7,6},{8,7},{9,8},{10,9},{11,1... | collective-permute-start | bytes 61448 | tf_op jit(solution)/shard_map/ppermute | solution.py:18
  22.5 5.7 %collective-permute-start = (bf16[16,2,320]{2,1,0:T(2,128)(2,1)}, bf16[16,2,320]{2,1,0:T(2,128)(2,1)S(1)}, u32[]{:S(2)}, u32[]{:S(2)}) collective-permute-start(bf16[16,2,320]{2,1,0:T(2,128)(2,1)} %get-tuple-element.98), channel_id=1, source_target_pairs={{0,1},{1,2},{2,3},{3,4},{4,5},{5,6},{6,7},{7,8},{8,9},{9,10},{10,1... | collective-permute-start | bytes 61448 | tf_op jit(solution)/shard_map/ppermute | solution.py:16
  29.7 1.8 pad_add_fusion
  36.3 20.6 %collective-permute-done.1 = bf16[16,2,320]{2,1,0:T(2,128)(2,1)S(1)} collective-permute-done((bf16[16,2,320]{2,1,0:T(2,128)(2,1)}, bf16[16,2,320]{2,1,0:T(2,128)(2,1)S(1)}, u32[]{:S(2)}, u32[]{:S(2)}) %collective-permute-start.1) | collective-permute-done | bytes 20512 | tf_op jit(solution)/shard_map/ppermute | solution.py:18
  73.3 2.8 %broadcast_in_dim.85 = bf16[16,9,20,320]{3,2,1,0:T(8,128)(2,1)} broadcast(bf16[9,20,320]{2,1,0:T(8,128)(2,1)} %param.25), dimensions={1,2,3} | broadcast | bytes 1958400 | tf_op jit(solution)/shard_map/broadcast_in_dim | solution.py:34
  76.1 9.4 %all-to-all-start.1 = ((bf16[16,9,20,320]{3,2,1,0:T(8,128)(2,1)}), bf16[16,9,20,320]{3,2,1,0:T(8,128)(2,1)}, u32[]{:S(2)}, u32[]{:S(2)}) async-start(bf16[16,9,20,320]{3,2,1,0:T(8,128)(2,1)} %broadcast_in_dim.85), calls=%async_computation.1 | async-start | bytes 5308416 | tf_op jit(solution)/shard_map/all_to_all | solution.py:33
  97.4 2.4 %reshape.348 = bf16[9,320,320]{2,1,0:T(8,128)(2,1)} reshape(bf16[9,16,20,320]{3,2,1,0:T(8,128)(2,1)S(1)} %copy.72) | data formatting | bytes 3686400 | tf_op jit(solution)/shard_map/reshape | solution.py:28
  99.8 3.6 %multiply_convert_fusion.2 = bf16[288,320]{1,0:T(8,128)(2,1)S(1)} fusion(bf16[288,9,320]{2,0,1:T(8,128)(2,1)} %constant_dynamic-update-slice_fusion.36, bf16[9,320,320]{2,1,0:T(8,128)(2,1)} %reshape.348), kind=kOutput, calls=%fused_computation.99 | convolution fusion | flops 531302400 | bytes 3686400 | tf_op jit(solution)/shard_map/tkc,kcd->td/dot_general | solution.py:63
  108.2 20.3 %all-to-all-done.1 = bf16[16,9,20,320]{3,2,1,0:T(8,128)(2,1)} async-done(((bf16[16,9,20,320]{3,2,1,0:T(8,128)(2,1)}), bf16[16,9,20,320]{3,2,1,0:T(8,128)(2,1)}, u32[]{:S(2)}, u32[]{:S(2)}) %all-to-all-start.1) | async-done | bytes 1843232 | tf_op jit(solution)/shard_map/all_to_all | solution.py:33
  128.5 2.1 %copy.82 = bf16[9,16,20,320]{3,2,1,0:T(8,128)(2,1)S(1)} copy(bf16[9,16,20,320]{3,2,0,1:T(8,128)(2,1)} %bitcast.76) | data formatting | bytes 3686400 | tf_op jit(solution)/shard_map/transpose | solution.py:26
  130.7 2.4 %reshape.350 = bf16[9,320,320]{2,1,0:T(8,128)(2,1)} reshape(bf16[9,16,20,320]{3,2,1,0:T(8,128)(2,1)S(1)} %copy.82) | data formatting | bytes 3686400 | tf_op jit(solution)/shard_map/reshape | solution.py:28
  139.1 2.2 %collective-permute-start.5 = (bf16[1,256,320]{1,2,0:T(8,128)(2,1)S(1)}, bf16[1,256,320]{1,2,0:T(8,128)(2,1)S(1)}, u32[]{:S(2)}, u32[]{:S(2)}) collective-permute-start(bf16[1,256,320]{1,2,0:T(8,128)(2,1)S(1)} %convert_bitcast_fusion), channel_id=1, source_target_pairs={{1,0},{2,1},{3,2},{4,3},{5,4},{6,5},{7,6},{8,7},{9,8},{10,9},{11,1... | collective-permute-start | bytes 491528 | tf_op jit(solution)/shard_map/ppermute | solution.py:18
  141.3 6.0 %collective-permute-start.4 = (bf16[1,256,320]{1,2,0:T(8,128)(2,1)S(1)}, bf16[1,256,320]{1,2,0:T(8,128)(2,1)S(1)}, u32[]{:S(2)}, u32[]{:S(2)}) collective-permute-start(bf16[1,256,320]{1,2,0:T(8,128)(2,1)S(1)} %convert_bitcast_fusion), channel_id=1, source_target_pairs={{0,1},{1,2},{2,3},{3,4},{4,5},{5,6},{6,7},{7,8},{8,9},{9,10},{10,1... | collective-permute-start | bytes 491528 | tf_op jit(solution)/shard_map/ppermute | solution.py:16
  151.6 2.1 gather_fusion
  156.3 4.3 %fusion.85 = (bf16[9,320,320]{2,0,1:T(8,128)(2,1)S(1)}, bf16[9,320,320]{2,0,1:T(8,128)(2,1)S(1)}) fusion(bf16[18,320,320]{2,0,1:T(8,128)(2,1)} %all-gather.2.cloned.1.call-done), kind=kLoop, calls=%fused_computation.160 | loop fusion | bytes 7372800 | tf_op jit(solution)/shard_map/split | solution.py:46
  161.1 1.9 copy.88
  163.0 5.5 %conditional.3 = (f32[16,16,320]{2,1,0:T(8,128)S(1)}) conditional(s32[]{:T(128)} %convert_element_type.80, () %tuple.22, (bf16[2,16,16,320]{3,2,1,0:T(8,128)(2,1)}, bf16[9,320,320]{2,1,0:T(8,128)(2,1)S(1)}, bf16[9,320,320]{2,1,0:T(8,128)(2,1)}) %tuple.25), branch_computations={%region_2.3_spmd, %region_3.4_spmd} | conditional | flops 944291840 | bytes 29955136 | solution.py:127
  168.6 5.5 %conditional.2 = (f32[16,16,320]{2,1,0:T(8,128)S(1)}) conditional(s32[]{:T(128)} %convert_element_type.79, () %tuple.20, (bf16[2,16,16,320]{3,2,1,0:T(8,128)(2,1)}, bf16[9,320,320]{2,1,0:T(8,128)(2,1)S(1)}, bf16[9,320,320]{2,1,0:T(8,128)(2,1)}) %tuple.25), branch_computations={%region_0.1_spmd, %region_1.2_spmd} | conditional | flops 944291840 | bytes 29955136 | solution.py:127
  174.9 1.9 collective-permute-start.3
  176.8 6.3 %collective-permute-start.2 = (bf16[2,256,320]{2,1,0:T(8,128)(2,1)}, bf16[2,256,320]{2,1,0:T(8,128)(2,1)}, u32[]{:S(2)}, u32[]{:S(2)}) collective-permute-start(bf16[2,256,320]{2,1,0:T(8,128)(2,1)} %pad_maximum_fusion.3), channel_id=1, source_target_pairs={{0,1},{1,2},{2,3},{3,4},{4,5},{5,6},{6,7},{7,8},{8,9},{9,10},{10,1... | collective-permute-start | bytes 983048 | tf_op jit(solution)/shard_map/ppermute | solution.py:16
  183.9 5.1 %fusion.92 = (f32[2,5,256]{2,1,0:T(8,128)S(1)}, f32[2,5,256,512]{3,2,1,0:T(8,128)}) fusion(bf16[2,512,5,64]{1,3,2,0:T(8,128)(2,1)} %bitcast.295, bf16[2,256,5,64]{1,0,3,2:T(2,128)(2,1)S(1)} %reshape.364), kind=kOutput, calls=%fused_computation.167 | convolution fusion | flops 171704832 | bytes 6236160 | tf_op jit(solution)/shard_map/sub | solution.py:154
  189.1 3.5 %fusion.46 = bf16[2,256,5,64]{1,3,2,0:T(8,128)(2,1)S(1)} fusion(bf16[2,512,5,64]{1,3,2,0:T(8,128)(2,1)S(1)} %bitcast.294, f32[2,5,256,512]{3,2,1,0:T(8,128)} %get-tuple-element.110, f32[2,5,256]{2,1,0:T(8,128)S(1)} %get-tuple-element.109), kind=kOutput, calls=%fused_computation.83 | convolution fusion | flops 170557440 | bytes 6236160 | tf_op jit(solution)/shard_map/shqk,skhd->sqhd/dot_general | solution.py:156
  202.8 2.4 %fusion.49 = bf16[5,64,256]{2,1,0:T(8,128)(2,1)S(1)} fusion(bf16[6,256,5,64]{1,3,2,0:T(8,128)(2,1)S(1)} %bitcast.248, f32[5,256]{1,0:T(8,128)S(1)} %exponential_add_fusion, f32[5,256]{1,0:T(8,128)S(1)} %broadcast_maximum_fusion, f32[5,6,256,256]{3,2,1,0:T(8,128)S(1)} %get-tuple-element.108, pred[6]{0:T(512)(128)(4,1)S(1)} %copy-done.19), kind=kOutput, calls=%fused_computation.88 | convolution fusion | flops 261570560 | bytes 9021446 | tf_op jit(solution)/shard_map/rhqgk,gkhd->rqhd/dot_general | solution.py:197
  (211 shorter events, 79.9 us)
Async XLA Ops:
  7.2 176.3 %copy-start = (bf16[320,320]{1,0:T(8,128)(2,1)S(1)}, bf16[320,320]{1,0:T(8,128)(2,1)}, u32[]{:S(2)}) copy-start(bf16[320,320]{1,0:T(8,128)(2,1)} %param.32) | copy-start | bytes 614404
  7.2 2.9 %copy-start.17 = (bf16[9,20,320]{2,1,0:T(8,128)(2,1)S(1)}, bf16[9,20,320]{2,1,0:T(8,128)(2,1)}, u32[]{:S(2)}) copy-start(bf16[9,20,320]{2,1,0:T(8,128)(2,1)} %param.24) | copy-start | bytes 345604
  7.2 149.1 %all-gather.2.cloned.1.call-start = ((), (), s32[]{:S(2)}) async-start(), calls=%async_computation.2 | async-start | bytes 6266880 | tf_op jit(solution)/shard_map/all_gather | solution.py:45
  11.9 7.7 %copy-start.7 = (bf16[16,16,320]{2,1,0:T(8,128)(2,1)S(1)}, bf16[16,16,320]{2,1,0:T(8,128)(2,1)}, u32[]{:S(2)}) copy-start(bf16[16,16,320]{2,1,0:T(8,128)(2,1)} %param.20) | copy-start | bytes 491524
  11.9 16.4 %copy-start.18 = (s32[32,2]{0,1:T(2,128)S(1)}, s32[32,2]{0,1:T(2,128)}, u32[]{:S(2)}) copy-start(s32[32,2]{0,1:T(2,128)} %param.23) | copy-start | bytes 772
  11.9 17.2 %copy-start.20 = (s32[16]{0:T(128)S(1)}, s32[16]{0:T(128)}, u32[]{:S(2)}) copy-start(s32[16]{0:T(128)} %param.22) | copy-start | bytes 196
  11.9 61.4 %all-to-all-start = ((bf16[16,9,20,320]{3,2,1,0:T(8,128)(2,1)}), bf16[16,9,20,320]{3,2,1,0:T(8,128)(2,1)S(1)}, u32[]{:S(2)}, u32[]{:S(2)}) async-start(bf16[16,9,20,320]{3,2,1,0:T(8,128)(2,1)} %broadcast_in_dim.83), calls=%async_computation | async-start | bytes 5308416 | tf_op jit(solution)/shard_map/all_to_all | solution.py:33
  20.3 36.6 %collective-permute-start.1 = (bf16[16,2,320]{2,1,0:T(2,128)(2,1)}, bf16[16,2,320]{2,1,0:T(2,128)(2,1)S(1)}, u32[]{:S(2)}, u32[]{:S(2)}) collective-permute-start(bf16[16,2,320]{2,1,0:T(2,128)(2,1)} %get-tuple-element.99), channel_id=1, source_target_pairs={{1,0},{2,1},{3,2},{4,3},{5,4},{6,5},{7,6},{8,7},{9,8},{10,9},{11,1... | collective-permute-start | bytes 61448 | tf_op jit(solution)/shard_map/ppermute | solution.py:18
  22.5 34.3 %collective-permute-start = (bf16[16,2,320]{2,1,0:T(2,128)(2,1)}, bf16[16,2,320]{2,1,0:T(2,128)(2,1)S(1)}, u32[]{:S(2)}, u32[]{:S(2)}) collective-permute-start(bf16[16,2,320]{2,1,0:T(2,128)(2,1)} %get-tuple-element.98), channel_id=1, source_target_pairs={{0,1},{1,2},{2,3},{3,4},{4,5},{5,6},{6,7},{7,8},{8,9},{9,10},{10,1... | collective-permute-start | bytes 61448 | tf_op jit(solution)/shard_map/ppermute | solution.py:16
  73.3 2.8 %copy-start.1 = (bf16[16,9,20,320]{3,2,1,0:T(8,128)(2,1)}, bf16[16,9,20,320]{3,2,1,0:T(8,128)(2,1)S(1)}, u32[]{:S(2)}) copy-start(bf16[16,9,20,320]{3,2,1,0:T(8,128)(2,1)S(1)} %all-to-all-done) | copy-start | bytes 5529604
  76.1 19.4 %copy-start.9 = (bf16[288,1,320]{2,0,1:T(8,128)(2,1)S(1)}, bf16[288,1,320]{2,0,1:T(8,128)(2,1)}, u32[]{:S(2)}) copy-start(bf16[288,1,320]{2,0,1:T(8,128)(2,1)} %stack.220) | copy-start | bytes 552964
  76.1 52.4 %all-to-all-start.1 = ((bf16[16,9,20,320]{3,2,1,0:T(8,128)(2,1)}), bf16[16,9,20,320]{3,2,1,0:T(8,128)(2,1)}, u32[]{:S(2)}, u32[]{:S(2)}) async-start(bf16[16,9,20,320]{3,2,1,0:T(8,128)(2,1)} %broadcast_in_dim.85), calls=%async_computation.1 | async-start | bytes 5308416 | tf_op jit(solution)/shard_map/all_to_all | solution.py:33
  85.5 11.5 %copy-start.2 = (bf16[16,9,20,320]{3,2,1,0:T(8,128)(2,1)S(1)}, bf16[16,9,20,320]{3,2,1,0:T(8,128)(2,1)}, u32[]{:S(2)}) copy-start(bf16[16,9,20,320]{3,2,1,0:T(8,128)(2,1)} %copy-done.1) | copy-start | bytes 5529604
  133.1 4.9 %copy-start.3 = (bf16[9,320,320]{2,1,0:T(8,128)(2,1)S(1)}, bf16[9,320,320]{2,1,0:T(8,128)(2,1)}, u32[]{:S(2)}) copy-start(bf16[9,320,320]{2,1,0:T(8,128)(2,1)} %reshape.350) | copy-start | bytes 5529604
  133.1 4.9 %copy-start.6 = (f32[256,320]{0,1:T(8,128)S(1)}, f32[256,320]{0,1:T(8,128)}, u32[]{:S(2)}) copy-start(f32[256,320]{0,1:T(8,128)} %copy.84) | copy-start | bytes 983044
  138.0 9.4 %copy-start.14 = (bf16[320,320]{1,0:T(8,128)(2,1)S(1)}, bf16[320,320]{1,0:T(8,128)(2,1)}, u32[]{:S(2)}) copy-start(bf16[320,320]{1,0:T(8,128)(2,1)} %param.28) | copy-start | bytes 614404
  139.0 10.8 %copy-start.22 = (bf16[320,320]{1,0:T(8,128)(2,1)S(1)}, bf16[320,320]{1,0:T(8,128)(2,1)}, u32[]{:S(2)}) copy-start(bf16[320,320]{1,0:T(8,128)(2,1)} %param.34) | copy-start | bytes 614404
  139.0 10.8 %copy-start.23 = (bf16[320,320]{1,0:T(8,128)(2,1)S(1)}, bf16[320,320]{1,0:T(8,128)(2,1)}, u32[]{:S(2)}) copy-start(bf16[320,320]{1,0:T(8,128)(2,1)} %param.33) | copy-start | bytes 614404
  139.1 9.3 %collective-permute-start.5 = (bf16[1,256,320]{1,2,0:T(8,128)(2,1)S(1)}, bf16[1,256,320]{1,2,0:T(8,128)(2,1)S(1)}, u32[]{:S(2)}, u32[]{:S(2)}) collective-permute-start(bf16[1,256,320]{1,2,0:T(8,128)(2,1)S(1)} %convert_bitcast_fusion), channel_id=1, source_target_pairs={{1,0},{2,1},{3,2},{4,3},{5,4},{6,5},{7,6},{8,7},{9,8},{10,9},{11,1... | collective-permute-start | bytes 491528 | tf_op jit(solution)/shard_map/ppermute | solution.py:18
  141.3 8.1 %collective-permute-start.4 = (bf16[1,256,320]{1,2,0:T(8,128)(2,1)S(1)}, bf16[1,256,320]{1,2,0:T(8,128)(2,1)S(1)}, u32[]{:S(2)}, u32[]{:S(2)}) collective-permute-start(bf16[1,256,320]{1,2,0:T(8,128)(2,1)S(1)} %convert_bitcast_fusion), channel_id=1, source_target_pairs={{0,1},{1,2},{2,3},{3,4},{4,5},{5,6},{6,7},{7,8},{8,9},{9,10},{10,1... | collective-permute-start | bytes 491528 | tf_op jit(solution)/shard_map/ppermute | solution.py:16
  174.9 19.6 %collective-permute-start.3 = (bf16[2,256,320]{2,1,0:T(8,128)(2,1)}, bf16[2,256,320]{2,1,0:T(8,128)(2,1)}, u32[]{:S(2)}, u32[]{:S(2)}) collective-permute-start(bf16[2,256,320]{2,1,0:T(8,128)(2,1)} %pad_maximum_fusion.3), channel_id=1, source_target_pairs={{1,0},{2,1},{3,2},{4,3},{5,4},{6,5},{7,6},{8,7},{9,8},{10,9},{11,1... | collective-permute-start | bytes 983048 | tf_op jit(solution)/shard_map/ppermute | solution.py:18
  176.8 17.7 %collective-permute-start.2 = (bf16[2,256,320]{2,1,0:T(8,128)(2,1)}, bf16[2,256,320]{2,1,0:T(8,128)(2,1)}, u32[]{:S(2)}, u32[]{:S(2)}) collective-permute-start(bf16[2,256,320]{2,1,0:T(8,128)(2,1)} %pad_maximum_fusion.3), channel_id=1, source_target_pairs={{0,1},{1,2},{2,3},{3,4},{4,5},{5,6},{6,7},{7,8},{8,9},{9,10},{10,1... | collective-permute-start | bytes 983048 | tf_op jit(solution)/shard_map/ppermute | solution.py:16
  183.9 5.1 %copy-start.10 = (bf16[2,512,320]{1,2,0:T(8,128)(2,1)S(1)}, bf16[2,512,320]{1,2,0:T(8,128)(2,1)}, u32[]{:S(2)}) copy-start(bf16[2,512,320]{1,2,0:T(8,128)(2,1)} %copy.117) | copy-start | bytes 1966084
  189.0 3.9 %copy-start.15 = (bf16[320,320]{1,0:T(8,128)(2,1)S(1)}, bf16[320,320]{1,0:T(8,128)(2,1)}, u32[]{:S(2)}) copy-start(bf16[320,320]{1,0:T(8,128)(2,1)} %param.35) | copy-start | bytes 614404
  (11 other events, 19.9 us)
Sparse Core Ops, SparseCore 0:
  11.9 113.5 all-gather.1
where the time goes:
time: 214 us; the launch traced here: 213 us
  local copies, waits for them, and re-layouts  77.1 us (36%)
  waiting for transfers between devices  42 us (20%)
  starting transfers between devices  41.5 us (19%)
  matrix products  25.8 us (12%)
  between operations  15.9 us (7%)
  other arithmetic  10.4 us (5%)
    unnamed x67, local copies, waits for them, and re-layouts  23.6 us
    ppermute x3, waiting for transfers between devices, padded_2(): lax.ppermute(head, axis, [((i + 1) % count, i) for i in range(count)])  20.6 us
    all_to_all x2, waiting for transfers between devices, sent_to_all(): lax.all_to_all(jnp.broadcast_to(array[None], (devices, *array.shape)), ax...  20.3 us
    another operation x24, local copies, waits for them, and re-layouts, tap_stack(): return jnp.stack(shifted, axis=3).reshape(-1, 9, padded.shape[-1])  18.6 us
    ppermute x3, starting transfers between devices, padded_2(): lax.ppermute(tail, axis, [(i, (i + 1) % count) for i in range(count)])  18 us
    all_to_all x2, starting transfers between devices, sent_to_all(): lax.all_to_all(jnp.broadcast_to(array[None], (devices, *array.shape)), ax...  17.1 us
    ppermute x3, starting transfers between devices, padded_2(): lax.ppermute(head, axis, [((i + 1) % count, i) for i in range(count)])  6.41 us
    sub x1, matrix products, body(): weights = jnp.exp(scores - highest)  5.12 us
  transfers between devices with their start and end apart: 9, of which 3 were waited for; matrix products, arithmetic and copies ran while one was open for 38% of the time, Pallas kernels for 0%

commit v1 on v0

v1 whole, which is shorter than its diff:
```python
import jax
import jax.numpy as jnp
import numpy as np
from jax import lax
from jax.experimental import pallas as pl
from jax.experimental.pallas import tpu as pltpu
from jax.sharding import PartitionSpec as P

MESH = pl.DeviceIdType.MESH
F32, BF = jnp.float32, jnp.bfloat16
HEADS, C, CP, TOK = 5, 320, 384, 256
SHARD = 192
NEG = -1e30

XP0, XP1, XM0, XM1, XP2, XM2 = range(6)
OPP, FAN, SIB, PER_PAIR = 6, 10, 22, 30
HALO, VIEWS, PANO, N_SEM = 60, 62, 64, 66


def rest_order(pair):
    order = [(0, 0), (1, 0), (0, 1), (1, 1), (0, 2), (1, 2), (2, 0), (2, 1), (2, 2)]
    return [3 * b + a if pair == 0 else 3 * a + b for a, b in order]


def tap_shift(pair, tap):
    return (tap % 3, tap // 3) if pair == 0 else (tap // 3, tap % 3)


def turn_matrix():
    m = np.zeros((TOK, TOK), np.float32)
    for r in range(TOK):
        m[r, (r % 16) * 16 + r // 16] = 1
    return m


def join_matrix():
    m = np.zeros((240, 256), np.float32)
    for r in range(240):
        tap, u = r // 80, r % 80
        m[r, (u // 20) * 64 + tap * 20 + u % 20] = 1
    return m


def kernel(
    wp, pano, views, count, links, turn, join,
    p2v_q, p2v_k, p2v_v, p2v_o, v2p_q, v2p_k, v2p_v, v2p_o,
    pano_out, view_out,
    sh, wm, wr, main, rc, r2, xpad, xext, vmid, pmid, vf, pf, wks, wvs, kv, vv, kp, vp, qs, att, ss, rs,
):
    s, f = lax.axis_index("slab"), lax.axis_index("frame")
    x, h, c = lax.div(s, 4), lax.rem(lax.div(s, 2), 2), lax.rem(s, 2)
    l, z = lax.div(f, 16), lax.rem(f, 16)
    xm, xp, xx = lax.rem(x + 3, 4), lax.rem(x + 1, 4), lax.rem(x + 2, 4)
    xs = (x, xm, xp, xx)

    def dev(x_, h_, c_, l_, z_):
        return (l_ * 16 + z_, x_ * 4 + h_ * 2 + c_)

    to_xp, to_xm = dev(xp, h, c, l, z), dev(xm, h, c, l, z)
    opposite, same = dev(x, 1 - h, c, 1 - l, z), dev(x, h, c, 1 - l, z)
    to_zp, to_zm = dev(x, h, c, l, lax.rem(z + 1, 16)), dev(x, h, c, l, lax.rem(z + 15, 16))
    sibling = dev(x, h, 1 - c, l, z)
    beyond = (f, lax.rem(s + 15 + 2 * c, 16))
    fans = (same, to_zp, to_zm)

    barrier = pltpu.get_barrier_semaphore()
    for d in (to_xp, to_xm, opposite, same, to_zp, to_zm, sibling, beyond):
        pl.semaphore_signal(barrier, inc=1, device_id=d, device_id_type=MESH)

    sent = []

    def copy(i, to, src, dst):
        return pltpu.make_async_remote_copy(
            src_ref=src, dst_ref=dst, send_sem=ss.at[i], recv_sem=rs.at[i], device_id=to, device_id_type=MESH
        )

    def send(i, to, src, dst=None):
        cp = copy(i, to, src, src if dst is None else dst)
        cp.start()
        sent.append(cp)

    def recv(i, dst):
        copy(i, sibling, dst, dst).wait_recv()

    def rows(q, x_, h_, c_, start, n):
        return sh.at[q, x_ * 4 + h_ * 2 + c_, pl.ds(start, n)]

    colour = lax.rem(z + 2 * l, 4)

    def quarter(q, x_, h_, k):
        return rows(q, x_, h_, c, pl.multiple_of(lax.rem(k, 4) * 48, 16), 48)

    def whole(q, x_, h_, c_):
        return sh.at[q, x_ * 4 + h_ * 2 + c_]

    def start_own(q):
        b = q * PER_PAIR
        send(b + XP0, to_xp, rows(q, x, h, c, 0, 96))
        send(b + XM0, to_xm, rows(q, x, h, c, 96, 96))
        send(b + XP1, to_xp, rows(q, x, h, c, 96, 96))
        send(b + XM1, to_xm, rows(q, x, h, c, 0, 96))
        send(b + OPP, opposite, quarter(q, x, h, colour + 2))
        send(b + SIB, sibling, whole(q, x, h, c))

    def second_hop(q):
        b = q * PER_PAIR
        recv(b + XP0, rows(q, xm, h, c, 0, 96))
        send(b + XP2, to_xp, rows(q, xm, h, c, 0, 96))
        recv(b + XM0, rows(q, xp, h, c, 96, 96))
        send(b + XM2, to_xm, rows(q, xp, h, c, 96, 96))

    def pass_on(q, j):
        b = q * PER_PAIR
        send(b + OPP + j, opposite, quarter(q, xs[j], h, colour + 2))
        send(b + SIB + j, sibling, whole(q, xs[j], h, c))

    def first_done(q):
        b = q * PER_PAIR
        recv(b + XP1, rows(q, xm, h, c, 96, 96))
        pass_on(q, 1)
        recv(b + XM1, rows(q, xp, h, c, 0, 96))
        pass_on(q, 2)

    def second_done(q):
        b = q * PER_PAIR
        recv(b + XP2, rows(q, xx, h, c, 0, 96))
        recv(b + XM2, rows(q, xx, h, c, 96, 96))
        pass_on(q, 3)

    def fan_out(q, j):
        b = q * PER_PAIR
        recv(b + OPP + j, quarter(q, xs[j], 1 - h, colour))
        for d in range(3):
            send(b + FAN + 4 * d + j, fans[d], quarter(q, xs[j], 1 - h, colour))

    def fanned(q, j):
        b = q * PER_PAIR
        for d, k in enumerate((2, 3, 1)):
            recv(b + FAN + 4 * d + j, quarter(q, xs[j], 1 - h, colour + k))
        send(b + SIB + 4 + j, sibling, whole(q, xs[j], 1 - h, c))

    def all_here(q):
        b = q * PER_PAIR
        for j in range(4):
            recv(b + SIB + j, whole(q, xs[j], h, 1 - c))
            recv(b + SIB + 4 + j, whole(q, xs[j], 1 - h, 1 - c))

    def dot(a, b):
        return jnp.dot(a, b, preferred_element_type=F32)

    def join_up(q):
        place = {tap: i for i, tap in enumerate(rest_order(q))}
        for x_ in range(4):
            for g in range(3):
                parts = jnp.concatenate([sh[q, 4 * x_ + i, 64 * g : 64 * g + 64, :] for i in range(4)], axis=0)
                joined = dot(join[...], parts).astype(BF)
                for k in range(3):
                    tap, block = 3 * g + k, joined[80 * k : 80 * k + 80]
                    if x_ < 3:
                        wm[q, 256 * tap + 80 * x_ : 256 * tap + 80 * x_ + 80, :] = block
                    else:
                        wm[q, 256 * tap + 240 : 256 * tap + 256, :] = block[:16]
                        wr[q, 64 * place[tap] : 64 * place[tap] + 64, :] = block[16:]

    def prepare(a, n):
        row = lax.broadcasted_iota(jnp.int32, (n, CP), 0) & 15
        moved = (
            jnp.where(row == 0, 0.0, pltpu.roll(a, 1, 0)),
            a,
            jnp.where(row == 15, 0.0, pltpu.roll(a, n - 1, 0)),
        )
        for i in range(3):
            main[i, :n, :] = moved[i][:, :256].astype(BF)
        t0, t1, t2 = (m[:, 256:] for m in moved)
        rc[:n, :] = (t0 + pltpu.roll(t1, 64, 1)).astype(BF)
        later = jnp.concatenate([t2[16:], t2[:16]], axis=0)
        r2[:n, :] = (t2 + pltpu.roll(later, 64, 1)).astype(BF)

    def conv(q, second, m):
        lo = 256 if second else 0
        left = []
        for tap in range(9):
            a, b = tap_shift(q, tap)
            left.append(main[a, 16 * b : 16 * b + m, :])
        acc = dot(jnp.concatenate(left, axis=1), wm[q, :, lo : lo + CP])
        rest = [rc[16 * b : 16 * b + m, :] for b in range(3)] + [r2[:m, :], r2[32 : 32 + m, :64]]
        acc += dot(jnp.concatenate(rest, axis=1), wr[q, :, lo : lo + CP])
        if second:
            acc = pltpu.roll(acc, C, 1)
        return jnp.where(lax.broadcasted_iota(jnp.int32, (m, CP), 1) < C, acc, 0.0)

    def silu(v):
        return v / (1.0 + jnp.exp(-v))

    def view_first(v):
        xpad[16:272, :C] = views[TOK * v : TOK * v + TOK, :].astype(F32)
        xpad[16:272, C:] = jnp.zeros((TOK, CP - C), F32)
        prepare(xpad[:288, :], 288)
        xpad[16:272, :] = silu(conv(0, False, TOK))

    def view_second(v):
        prepare(xpad[:288, :], 288)
        acc = conv(0, True, TOK)
        vmid[v, :, :] = acc
        vmid[v, :, :C] = acc[:, :C] + views[TOK * v : TOK * v + TOK, :].astype(F32)

    def put_values(to, g, val):
        val = val.astype(BF)
        to[g, :, 0:128] = val[:, :128]
        to[g, :, 256:384] = val[:, 128:256]
        to[g, :, 512:576] = val[:, 256:320]

    def view_pairs(o):
        first, second = vf[o, :, :C], vf[o, :, 256:]
        kv[2 * o, :, :C] = dot(first, p2v_k[...]).astype(BF)
        put_values(vv, 2 * o, dot(first, p2v_v[...]))
        kv[2 * o + 1, :, :C] = dot(second, wks[...]).astype(BF)
        put_values(vv, 2 * o + 1, dot(second, wvs[...]))

    def pano_pairs(o):
        feat = pf[o, :, :C]
        kp[o, :, :C] = dot(feat, v2p_k[...]).astype(BF)
        put_values(vp, o, dot(feat, v2p_v[...]))

    def attend(keys, values, bias, sink):
        lane = lax.broadcasted_iota(jnp.int32, (TOK, 128), 1)
        for j in range(3):
            query, ks = qs[:, 128 * j : 128 * j + 128], keys(j)
            vs = jnp.concatenate(values(j), axis=0)
            halves = []
            for e in range(2 if j < 2 else 1):
                mine = (lane >= 64 * e) & (lane < 64 * e + 64)
                picked = jnp.where(mine, query, jnp.zeros_like(query))
                scores = [
                    lax.dot_general(picked, k, (((1,), (1,)), ((), ())), preferred_element_type=F32) for k in ks
                ]
                top = None
                for sc, b in zip(scores, bias, strict=True):
                    t = jnp.max(sc, axis=1, keepdims=True)
                    t = t if b is None else t + b
                    top = t if top is None else jnp.maximum(top, t)
                if sink:
                    top = jnp.maximum(top, 0.0)
                shares = [
                    jnp.exp(sc - (top if b is None else top - b)).astype(BF) for sc, b in zip(scores, bias, strict=True)
                ]
                both = dot(jnp.concatenate(shares, axis=1), vs)
                total = both[:, 128:]
                if sink:
                    total = total + jnp.exp(-top)
                halves.append(both[:, :128] / total)
            out = halves[0] if j == 2 else jnp.where(lane < 64, halves[0], halves[1])
            att[:, 128 * j : 128 * j + 128] = out.astype(BF)

    sh[0, s] = wp[0]
    sh[1, s] = wp[1]
    xext[32:288, 256:] = jnp.zeros((TOK, 128), BF)
    xext[32:288, :C] = dot(turn[...], pano[...]).astype(BF)
    pl.semaphore_wait(barrier, 8)
    start_own(0)
    send(HALO, sibling, xext.at[pl.ds(pl.multiple_of(32 + 224 * (1 - c), 16), 32)],
         xext.at[pl.ds(pl.multiple_of(288 * c, 16), 32)])
    send(HALO + 1, beyond, xext.at[pl.ds(pl.multiple_of(32 + 224 * c, 16), 32)],
         xext.at[pl.ds(pl.multiple_of(288 * (1 - c), 16), 32)])

    xpad[0:16, :] = jnp.zeros((16, CP), F32)
    xpad[272:288, :] = jnp.zeros((16, CP), F32)
    for buf, n in ((kv, 6), (kp, 3)):
        for g in range(n):
            buf[g, :, 256:] = jnp.zeros((TOK, 128), BF)
    for buf, n in ((vv, 6), (vp, 3)):
        for g in range(n):
            for j in range(3):
                buf[g, :, 256 * j + 128 : 256 * j + 256] = jnp.ones((TOK, 128), BF)
            buf[g, :, 512:640] = jnp.zeros((TOK, 128), BF)
    qs[:, 256:] = jnp.zeros((TOK, 128), BF)
    for to, w in ((wks, p2v_k), (wvs, p2v_v)):
        to[0:64, :] = jnp.zeros((64, C), BF)
        to[64:384, :] = w[...]

    second_hop(0)
    start_own(1)
    first_done(0)
    for j in range(3):
        fan_out(0, j)
    second_done(0)
    fan_out(0, 3)
    second_hop(1)
    for j in range(4):
        fanned(0, j)
    first_done(1)
    all_here(0)

    join_up(0)
    view_first(0)
    fan_out(1, 0)
    fan_out(1, 1)
    fan_out(1, 2)
    view_second(0)
    second_done(1)
    view_first(1)
    fan_out(1, 3)
    for j in range(3):
        fanned(1, j)
    view_second(1)
    fanned(1, 3)
    f0, f1 = vmid[0], pltpu.roll(vmid[1], 64, 1)
    vf[1, :, :256] = f0[:, :256].astype(BF)
    vf[1, :, 256:384] = (f0[:, 256:] + f1[:, :128]).astype(BF)
    vf[1, :, 384:] = f1[:, 128:].astype(BF)
    send(VIEWS, sibling, vf.at[1], vf.at[2 * c])
    send(VIEWS + 1, beyond, vf.at[1], vf.at[2 * (1 - c)])
    view_pairs(1)

    recv(HALO, xext.at[pl.ds(pl.multiple_of(288 * (1 - c), 16), 32)])
    recv(HALO + 1, xext.at[pl.ds(pl.multiple_of(288 * c, 16), 32)])
    prepare(xext[...].astype(F32), 320)
    all_here(1)
    join_up(1)
    hidden = silu(conv(1, False, 288))
    prepare(hidden, 288)
    mid = conv(1, True, TOK) + xext[32:288, :].astype(F32)
    pmid[...] = mid
    pf[1] = mid.astype(BF)
    send(PANO, sibling, pf.at[1], pf.at[2 * c])
    send(PANO + 1, beyond, pf.at[1], pf.at[2 * (1 - c)])
    pano_pairs(1)

    recv(VIEWS, vf.at[2 * (1 - c)])
    recv(VIEWS + 1, vf.at[2 * c])
    view_pairs(0)
    view_pairs(2)
    qs[:, :C] = (dot(pf[1, :, :C], p2v_q[...]).astype(BF).astype(F32) * 0.125).astype(BF)
    bias = []
    for o in range(3):
        so = lax.rem(s + 15 + o, 16)
        for v in range(2):
            named = (links[2 * so + v, 0] == 2 - o) | (links[2 * so + v, 1] == 2 - o)
            bias.append(jnp.where(named & (count[so] > v), 0.0, NEG))
    attend(
        lambda j: [kv[g, :, 128 * j : 128 * j + 128] for g in range(6)],
        lambda j: [vv[g, :, 256 * j : 256 * j + 256] for g in range(6)],
        bias,
        True,
    )
    total = pmid[:, :C] + dot(att[:, :C], p2v_o[...])
    pano_out[...] = dot(turn[...], total.astype(BF)).astype(BF)

    recv(PANO, pf.at[2 * (1 - c)])
    recv(PANO + 1, pf.at[2 * c])
    pano_pairs(0)
    pano_pairs(2)
    for v in range(2):
        feat = vmid[v, :, :C].astype(BF)
        qs[:, :C] = (dot(feat, v2p_q[...]).astype(BF).astype(F32) * 0.125).astype(BF)
        a, b = links[2 * s + v, 0], links[2 * s + v, 1]
        attend(
            lambda j: [kp[i, :, 128 * j : 128 * j + 128] for i in (a, b)],
            lambda j: [vp[i, :, 256 * j : 256 * j + 256] for i in (a, b)],
            [None, None],
            False,
        )
        total = vmid[v, :, :C] + dot(att[:, :C], v2p_o[...])
        total = total * jnp.where(count[s] > v, 1.0, 0.0)
        view_out[TOK * v : TOK * v + TOK, :] = total.astype(BF)

    for cp in sent:
        cp.wait_send()


def packed(first, second):
    both = jnp.concatenate([first, second], axis=2).reshape(3, 60, 2 * C)
    return jnp.pad(both, ((0, 0), (0, 4), (0, 0))).reshape(SHARD, 2 * C)


def body(pano, views, count, links, pc1, pc2, vc1, vc2, *projections):
    wp = jnp.stack([packed(vc1, vc2), packed(pc1, pc2)])
    vmem, smem = pl.BlockSpec(memory_space=pltpu.VMEM), pl.BlockSpec(memory_space=pltpu.SMEM)
    pano_out, view_out = pl.pallas_call(
        kernel,
        out_shape=(jax.ShapeDtypeStruct((TOK, C), BF), jax.ShapeDtypeStruct((2 * TOK, C), BF)),
        in_specs=[vmem] * 3 + [smem] * 2 + [vmem] * 10,
        out_specs=(vmem, vmem),
        scratch_shapes=[
            pltpu.VMEM((2, 16, SHARD, 2 * C), BF),
            pltpu.VMEM((2, 9 * 256, 2 * C), BF),
            pltpu.VMEM((2, 9 * 64, 2 * C), BF),
            pltpu.VMEM((3, 320, 256), BF),
            pltpu.VMEM((320, 128), BF),
            pltpu.VMEM((320, 128), BF),
            pltpu.VMEM((288, CP), F32),
            pltpu.VMEM((320, CP), BF),
            pltpu.VMEM((2, TOK, CP), F32),
            pltpu.VMEM((TOK, CP), F32),
            pltpu.VMEM((3, TOK, 2 * C), BF),
            pltpu.VMEM((3, TOK, CP), BF),
            pltpu.VMEM((CP, C), BF),
            pltpu.VMEM((CP, C), BF),
            pltpu.VMEM((6, TOK, CP), BF),
            pltpu.VMEM((6, TOK, 768), BF),
            pltpu.VMEM((3, TOK, CP), BF),
            pltpu.VMEM((3, TOK, 768), BF),
            pltpu.VMEM((TOK, CP), BF),
            pltpu.VMEM((TOK, CP), BF),
            pltpu.SemaphoreType.DMA((N_SEM,)),
            pltpu.SemaphoreType.DMA((N_SEM,)),
        ],
        compiler_params=pltpu.CompilerParams(
            collective_id=0, has_side_effects=True, vmem_limit_bytes=56 * 1024 * 1024
        ),
    )(
        wp, pano.reshape(TOK, C), views.reshape(2 * TOK, C), count, links,
        jnp.asarray(turn_matrix(), BF), jnp.asarray(join_matrix(), BF), *projections,
    )
    return pano_out.reshape(pano.shape), view_out.reshape(views.shape)


def solution(mesh):
    in_specs = (
        P("frame", "slab", None),
        P(("frame", "slab"), None, None, None),
        P("frame"),
        P("frame", None),
        *[P(None, "slab", None)] * 4,
        *[P()] * 8,
    )
    out_specs = (P("frame", "slab", None), P(("frame", "slab"), None, None, None))
    return jax.shard_map(body, mesh=mesh, in_specs=in_specs, out_specs=out_specs, check_vma=False)
```

time: 214 us -> 76.3 us (0.36)
  the two profiles are of different devices: /device:TPU:497 before, /device:TPU:3 now
where the time goes in v1:
time: 76.3 us; the launch traced here: 76.1 us
  Pallas kernels  68.5 us (90%)
  local copies, waits for them, and re-layouts  4.87 us (6%)
  other arithmetic  2.07 us (3%)
    pallas_call x1, Pallas kernels, body(): pl.pallas_call(kernel, out_shape=(jax.ShapeDtypeStruct((TOK, C), BF), jax...  68.5 us
    unnamed x11, local copies, waits for them, and re-layouts  4.74 us

profile of v1, /device:TPU:3, one launch (start us, length us, event | category | flops | bytes accessed | tf_op | source)
XLA Modules:
  0.0 76.1 jit_solution(8037529861683868320)
XLA Ops:
  0.6 0.0 copy-start.3
  0.6 0.7 copy-done.3
  1.3 0.7 copy.20.links
  2.0 1.1 %pad_maximum_fusion.2 = bf16[9,20,640]{2,1,0:T(8,128)(2,1)S(1)} fusion(bf16[9,20,320]{2,1,0:T(8,128)(2,1)} %param.23, bf16[9,20,320]{2,1,0:T(8,128)(2,1)} %param.22), kind=kLoop, calls=%fused_computation.2 | loop fusion | flops 460800 | bytes 460800 | tf_op jit(solution)/shard_map/concatenate | solution.py:372
  3.2 0.0 copy-start.1
  3.2 0.0 copy-start.2
  3.2 0.9 %copy-done.1 = bf16[9,20,320]{2,1,0:T(8,128)(2,1)S(1)} copy-done((bf16[9,20,320]{2,1,0:T(8,128)(2,1)S(1)}, bf16[9,20,320]{2,1,0:T(8,128)(2,1)}, u32[]{:S(2)}) %copy-start.1) | copy-done | bytes 115224
  4.1 0.1 copy-done.2
  4.2 0.1 pad_maximum_fusion.1
  4.4 0.8 %pad_maximum_fusion.wp = bf16[2,192,640]{2,1,0:T(8,128)(2,1)} fusion(bf16[1,192,640]{2,1,0:T(8,128)(2,1)S(1)} %bitcast.6, bf16[1,192,640]{2,1,0:T(8,128)(2,1)S(1)} %bitcast.7), kind=kLoop, calls=%fused_computation | loop fusion | flops 245760 | bytes 983040 | tf_op jit(solution)/shard_map/stack | solution.py:377
  5.2 68.5 %shard_map.185 = (bf16[256,320]{1,0:T(8,128)(2,1)}, bf16[512,320]{1,0:T(8,128)(2,1)}) custom-call(bf16[2,192,640]{2,1,0:T(8,128)(2,1)} %pad_maximum_fusion.wp, bf16[256,320]{1,0:T(8,128)(2,1)} %bitcast.10, bf16[512,320]{1,0:T(8,128)(2,1)} %bitcast.9, s32[16]{0:T(128)} %count.1, s32[32,2]{1,0:T(8,128)} %copy.20.links, bf16[256,256]{1,0:T(8,128)(2,1)} %constant.7.clone.turn, ...), custom_call_target="tpu_custom_call" | custom-call | tf_op jit(solution)/shard_map/pallas_call | solution.py:379
  73.7 0.0 copy-start
  73.7 1.7 %copy.23 = bf16[16,16,320]{2,1,0:T(8,128)(2,1)} copy(bf16[16,16,320]{2,1,0:T(8,128)(2,1)} %bitcast.11) | data formatting | bytes 327680
  75.3 0.0 copy-done
  75.4 0.7 copy.24
  (4 shorter events, 0.1 us)
Async XLA Ops:
  0.6 0.7 copy-start.3
  3.2 0.9 %copy-start.1 = (bf16[9,20,320]{2,1,0:T(8,128)(2,1)S(1)}, bf16[9,20,320]{2,1,0:T(8,128)(2,1)}, u32[]{:S(2)}) copy-start(bf16[9,20,320]{2,1,0:T(8,128)(2,1)} %param.25) | copy-start | bytes 345604
  3.2 1.0 %copy-start.2 = (bf16[9,20,320]{2,1,0:T(8,128)(2,1)S(1)}, bf16[9,20,320]{2,1,0:T(8,128)(2,1)}, u32[]{:S(2)}) copy-start(bf16[9,20,320]{2,1,0:T(8,128)(2,1)} %param.24) | copy-start | bytes 345604
  73.7 1.7 %copy-start = (bf16[512,320]{1,0:T(8,128)(2,1)S(1)}, bf16[512,320]{1,0:T(8,128)(2,1)}, u32[]{:S(2)}) copy-start(bf16[512,320]{1,0:T(8,128)(2,1)} %get-tuple-element.5) | copy-start | bytes 983044

commit v2 on v1

--- a/solution.py
+++ b/solution.py
@@ -42,7 +42,7 @@
 
 
 def kernel(
-    wp, pano, views, count, links, turn, join,
+    pc1, pc2, vc1, vc2, pano, views, count, links, turn, join, spread,
     p2v_q, p2v_k, p2v_v, p2v_o, v2p_q, v2p_k, v2p_v, v2p_o,
     pano_out, view_out,
     sh, wm, wr, main, rc, r2, xpad, xext, vmid, pmid, vf, pf, wks, wvs, kv, vv, kp, vp, qs, att, ss, rs,
@@ -144,6 +144,18 @@
         for j in range(4):
             recv(b + SIB + j, whole(q, xs[j], h, 1 - c))
             recv(b + SIB + 4 + j, whole(q, xs[j], 1 - h, 1 - c))
+
+    def pack(q, first, second):
+        for g in range(3):
+            for i, w in enumerate((first, second)):
+                xpad[64 * i : 64 * i + 64, :C] = sum(
+                    dot(spread[64 * k : 64 * k + 64, :], w[3 * g + k]) for k in range(3)
+                )
+            moved = pltpu.roll(xpad[64:128, :], 64, 1)
+            at = slice(64 * g, 64 * g + 64)
+            sh[q, s, at, :256] = xpad[0:64, :256].astype(BF)
+            sh[q, s, at, 256:384] = (xpad[0:64, 256:] + moved[:, :128]).astype(BF)
+            sh[q, s, at, 384:] = moved[:, 128:].astype(BF)
 
     def dot(a, b):
         return jnp.dot(a, b, preferred_element_type=F32)
@@ -252,8 +264,8 @@
             out = halves[0] if j == 2 else jnp.where(lane < 64, halves[0], halves[1])
             att[:, 128 * j : 128 * j + 128] = out.astype(BF)
 
-    sh[0, s] = wp[0]
-    sh[1, s] = wp[1]
+    xpad[0:128, 256:] = jnp.zeros((128, 128), F32)
+    pack(0, vc1, vc2)
     xext[32:288, 256:] = jnp.zeros((TOK, 128), BF)
     xext[32:288, :C] = dot(turn[...], pano[...]).astype(BF)
     pl.semaphore_wait(barrier, 8)
@@ -263,6 +275,7 @@
     send(HALO + 1, beyond, xext.at[pl.ds(pl.multiple_of(32 + 224 * c, 16), 32)],
          xext.at[pl.ds(pl.multiple_of(288 * (1 - c), 16), 32)])
 
+    pack(1, pc1, pc2)
     xpad[0:16, :] = jnp.zeros((16, CP), F32)
     xpad[272:288, :] = jnp.zeros((16, CP), F32)
     for buf, n in ((kv, 6), (kp, 3)):
@@ -280,30 +293,31 @@
 
     second_hop(0)
     start_own(1)
+    fan_out(0, 0)
     first_done(0)
-    for j in range(3):
-        fan_out(0, j)
     second_done(0)
+    fan_out(0, 1)
+    fan_out(0, 2)
     fan_out(0, 3)
     second_hop(1)
+    fan_out(1, 0)
     for j in range(4):
         fanned(0, j)
     first_done(1)
-    all_here(0)
-
-    join_up(0)
-    view_first(0)
-    fan_out(1, 0)
     fan_out(1, 1)
     fan_out(1, 2)
-    view_second(0)
+    all_here(0)
+
+    join_up(0)
     second_done(1)
-    view_first(1)
+    view_first(0)
     fan_out(1, 3)
     for j in range(3):
         fanned(1, j)
+    view_second(0)
+    fanned(1, 3)
+    view_first(1)
     view_second(1)
-    fanned(1, 3)
     f0, f1 = vmid[0], pltpu.roll(vmid[1], 64, 1)
     vf[1, :, :256] = f0[:, :256].astype(BF)
     vf[1, :, 256:384] = (f0[:, 256:] + f1[:, :128]).astype(BF)
@@ -368,18 +382,20 @@
         cp.wait_send()
 
 
-def packed(first, second):
-    both = jnp.concatenate([first, second], axis=2).reshape(3, 60, 2 * C)
-    return jnp.pad(both, ((0, 0), (0, 4), (0, 0))).reshape(SHARD, 2 * C)
+def spread_matrix():
+    m = np.zeros((192, 20), np.float32)
+    for k in range(3):
+        for j in range(20):
+            m[64 * k + 20 * k + j, j] = 1
+    return m
 
 
 def body(pano, views, count, links, pc1, pc2, vc1, vc2, *projections):
-    wp = jnp.stack([packed(vc1, vc2), packed(pc1, pc2)])
     vmem, smem = pl.BlockSpec(memory_space=pltpu.VMEM), pl.BlockSpec(memory_space=pltpu.SMEM)
     pano_out, view_out = pl.pallas_call(
         kernel,
         out_shape=(jax.ShapeDtypeStruct((TOK, C), BF), jax.ShapeDtypeStruct((2 * TOK, C), BF)),
-        in_specs=[vmem] * 3 + [smem] * 2 + [vmem] * 10,
+        in_specs=[vmem] * 6 + [smem] * 2 + [vmem] * 11,
         out_specs=(vmem, vmem),
         scratch_shapes=[
             pltpu.VMEM((2, 16, SHARD, 2 * C), BF),
@@ -409,8 +425,8 @@
             collective_id=0, has_side_effects=True, vmem_limit_bytes=56 * 1024 * 1024
         ),
     )(
-        wp, pano.reshape(TOK, C), views.reshape(2 * TOK, C), count, links,
-        jnp.asarray(turn_matrix(), BF), jnp.asarray(join_matrix(), BF), *projections,
+        pc1, pc2, vc1, vc2, pano.reshape(TOK, C), views.reshape(2 * TOK, C), count, links,
+        jnp.asarray(turn_matrix(), BF), jnp.asarray(join_matrix(), BF), jnp.asarray(spread_matrix(), BF), *projections,
     )
     return pano_out.reshape(pano.shape), view_out.reshape(views.shape)
 

time: 76.3 us -> 73.4 us (0.962)
  the two profiles are of different devices: /device:TPU:3 before, /device:TPU:7 now
where the time goes in v2:
time: 73.4 us; the launch traced here: 73.3 us
  Pallas kernels  68.8 us (94%)
  local copies, waits for them, and re-layouts  3.79 us (5%)
    pallas_call x1, Pallas kernels, body(): pl.pallas_call(kernel, out_shape=(jax.ShapeDtypeStruct((TOK, C), BF), jax...  68.8 us
    unnamed x7, local copies, waits for them, and re-layouts  3.79 us

profile of v2, /device:TPU:7, one launch (start us, length us, event | category | flops | bytes accessed | tf_op | source)
XLA Modules:
  0.0 73.3 jit_solution(11049018436671333760)
XLA Ops:
  0.6 0.0 copy-start.1
  0.6 0.7 copy-done.1
  1.3 0.7 copy.21.links
  2.0 68.8 %shard_map.194 = (bf16[256,320]{1,0:T(8,128)(2,1)}, bf16[512,320]{1,0:T(8,128)(2,1)}) custom-call(bf16[9,20,320]{2,1,0:T(8,128)(2,1)} %pc1.1, bf16[9,20,320]{2,1,0:T(8,128)(2,1)} %pc2.1, bf16[9,20,320]{2,1,0:T(8,128)(2,1)} %vc1.1, bf16[9,20,320]{2,1,0:T(8,128)(2,1)} %vc2.1, bf16[256,320]{1,0:T(8,128)(2,1)} %bitcast.7, bf16[512,320]{1,0:T(8,128)(2,1)} %bitcast.5, ...), custom_call_target="tpu_custom_call" | custom-call | tf_op jit(solution)/shard_map/pallas_call | solution.py:395
  70.8 0.0 copy-start
  70.8 1.7 %copy.24 = bf16[16,16,320]{2,1,0:T(8,128)(2,1)} copy(bf16[16,16,320]{2,1,0:T(8,128)(2,1)} %bitcast.6) | data formatting | bytes 327680
  72.5 0.0 copy-done
  72.5 0.7 %copy.25 = bf16[2,16,16,320]{3,2,1,0:T(8,128)(2,1)} copy(bf16[2,16,16,320]{3,2,1,0:T(8,128)(2,1)S(1)} %bitcast.4) | data formatting | bytes 655360
Async XLA Ops:
  0.6 0.7 copy-start.1
  70.8 1.7 %copy-start = (bf16[512,320]{1,0:T(8,128)(2,1)S(1)}, bf16[512,320]{1,0:T(8,128)(2,1)}, u32[]{:S(2)}) copy-start(bf16[512,320]{1,0:T(8,128)(2,1)} %get-tuple-element.5) | copy-start | bytes 983044

commit v3 on v2

--- a/solution.py
+++ b/solution.py
@@ -14,7 +14,7 @@
 
 XP0, XP1, XM0, XM1, XP2, XM2 = range(6)
 OPP, FAN, SIB, PER_PAIR = 6, 10, 22, 30
-HALO, VIEWS, PANO, N_SEM = 60, 62, 64, 66
+HALO, VIEWS, PANO, N_SEM = 60, 62, 66, 68
 
 
 def rest_order(pair):
@@ -264,6 +264,13 @@
             out = halves[0] if j == 2 else jnp.where(lane < 64, halves[0], halves[1])
             att[:, 128 * j : 128 * j + 128] = out.astype(BF)
 
+    def view_part(o, part):
+        return vf.at[o, :, pl.ds(256, CP)] if part else vf.at[o, :, pl.ds(0, 256)]
+
+    def send_views(part):
+        send(VIEWS + 2 * part, sibling, view_part(1, part), view_part(2 * c, part))
+        send(VIEWS + 2 * part + 1, beyond, view_part(1, part), view_part(2 * (1 - c), part))
+
     xpad[0:128, 256:] = jnp.zeros((128, 128), F32)
     pack(0, vc1, vc2)
     xext[32:288, 256:] = jnp.zeros((TOK, 128), BF)
@@ -315,15 +322,15 @@
     for j in range(3):
         fanned(1, j)
     view_second(0)
+    vf[1, :, :256] = vmid[0, :, :256].astype(BF)
+    send_views(0)
     fanned(1, 3)
     view_first(1)
     view_second(1)
-    f0, f1 = vmid[0], pltpu.roll(vmid[1], 64, 1)
-    vf[1, :, :256] = f0[:, :256].astype(BF)
-    vf[1, :, 256:384] = (f0[:, 256:] + f1[:, :128]).astype(BF)
+    f1 = pltpu.roll(vmid[1], 64, 1)
+    vf[1, :, 256:384] = (vmid[0, :, 256:] + f1[:, :128]).astype(BF)
     vf[1, :, 384:] = f1[:, 128:].astype(BF)
-    send(VIEWS, sibling, vf.at[1], vf.at[2 * c])
-    send(VIEWS + 1, beyond, vf.at[1], vf.at[2 * (1 - c)])
+    send_views(1)
     view_pairs(1)
 
     recv(HALO, xext.at[pl.ds(pl.multiple_of(288 * (1 - c), 16), 32)])
@@ -340,8 +347,9 @@
     send(PANO + 1, beyond, pf.at[1], pf.at[2 * (1 - c)])
     pano_pairs(1)
 
-    recv(VIEWS, vf.at[2 * (1 - c)])
-    recv(VIEWS + 1, vf.at[2 * c])
+    for part in range(2):
+        recv(VIEWS + 2 * part, view_part(2 * (1 - c), part))
+        recv(VIEWS + 2 * part + 1, view_part(2 * c, part))
     view_pairs(0)
     view_pairs(2)
     qs[:, :C] = (dot(pf[1, :, :C], p2v_q[...]).astype(BF).astype(F32) * 0.125).astype(BF)

time: 73.4 us -> 72.9 us (level)
  the two profiles are of different devices: /device:TPU:7 before, /device:TPU:1 now
where the time goes in v3:
time: 72.9 us; the launch traced here: 72.8 us
  Pallas kernels  68.3 us (94%)
  local copies, waits for them, and re-layouts  3.79 us (5%)
    pallas_call x1, Pallas kernels, body(): pl.pallas_call(kernel, out_shape=(jax.ShapeDtypeStruct((TOK, C), BF), jax...  68.3 us
    unnamed x7, local copies, waits for them, and re-layouts  3.79 us

profile of v3, /device:TPU:1, one launch (start us, length us, event | category | flops | bytes accessed | tf_op | source)
XLA Modules:
  0.0 72.8 jit_solution(10169451520674848072)
XLA Ops:
  0.6 0.0 copy-start.1
  0.6 0.7 copy-done.1
  1.3 0.7 copy.21.links
  2.0 68.3 %shard_map.194 = (bf16[256,320]{1,0:T(8,128)(2,1)}, bf16[512,320]{1,0:T(8,128)(2,1)}) custom-call(bf16[9,20,320]{2,1,0:T(8,128)(2,1)} %pc1.1, bf16[9,20,320]{2,1,0:T(8,128)(2,1)} %pc2.1, bf16[9,20,320]{2,1,0:T(8,128)(2,1)} %vc1.1, bf16[9,20,320]{2,1,0:T(8,128)(2,1)} %vc2.1, bf16[256,320]{1,0:T(8,128)(2,1)} %bitcast.7, bf16[512,320]{1,0:T(8,128)(2,1)} %bitcast.5, ...), custom_call_target="tpu_custom_call" | custom-call | tf_op jit(solution)/shard_map/pallas_call | solution.py:403
  70.3 0.0 copy-start
  70.3 1.7 %copy.24 = bf16[16,16,320]{2,1,0:T(8,128)(2,1)} copy(bf16[16,16,320]{2,1,0:T(8,128)(2,1)} %bitcast.6) | data formatting | bytes 327680
  72.0 0.0 copy-done
  72.0 0.7 %copy.25 = bf16[2,16,16,320]{3,2,1,0:T(8,128)(2,1)} copy(bf16[2,16,16,320]{3,2,1,0:T(8,128)(2,1)S(1)} %bitcast.4) | data formatting | bytes 655360
Async XLA Ops:
  0.6 0.7 copy-start.1
  70.3 1.7 %copy-start = (bf16[512,320]{1,0:T(8,128)(2,1)S(1)}, bf16[512,320]{1,0:T(8,128)(2,1)}, u32[]{:S(2)}) copy-start(bf16[512,320]{1,0:T(8,128)(2,1)} %get-tuple-element.5) | copy-start | bytes 983044

commit v4 on v3

--- a/solution.py
+++ b/solution.py
@@ -299,9 +299,9 @@
         to[64:384, :] = w[...]
 
     second_hop(0)
-    start_own(1)
     fan_out(0, 0)
     first_done(0)
+    start_own(1)
     second_done(0)
     fan_out(0, 1)
     fan_out(0, 2)

time: 72.9 us -> 76 us (1.043)
  Pallas kernels: 68.3 us -> 71.4 us
    pallas_call x1, Pallas kernels: 68.3 us -> 71.4 us  [body(): pl.pallas_call(kernel, out_shape=(jax.ShapeDtypeStruct((TOK, C), BF), jax...]
where the time goes in v4:
time: 76 us; the launch traced here: 75.8 us
  Pallas kernels  71.4 us (94%)
  local copies, waits for them, and re-layouts  3.79 us (5%)
    pallas_call x1, Pallas kernels, body(): pl.pallas_call(kernel, out_shape=(jax.ShapeDtypeStruct((TOK, C), BF), jax...  71.4 us
    unnamed x7, local copies, waits for them, and re-layouts  3.79 us

profile of v4, /device:TPU:1, one launch (start us, length us, event | category | flops | bytes accessed | tf_op | source)
XLA Modules:
  0.0 75.8 jit_solution(13398467238913862938)
XLA Ops:
  0.6 0.0 copy-start.1
  0.6 0.7 copy-done.1
  1.3 0.7 copy.21.links
  2.0 71.4 %shard_map.194 = (bf16[256,320]{1,0:T(8,128)(2,1)}, bf16[512,320]{1,0:T(8,128)(2,1)}) custom-call(bf16[9,20,320]{2,1,0:T(8,128)(2,1)} %pc1.1, bf16[9,20,320]{2,1,0:T(8,128)(2,1)} %pc2.1, bf16[9,20,320]{2,1,0:T(8,128)(2,1)} %vc1.1, bf16[9,20,320]{2,1,0:T(8,128)(2,1)} %vc2.1, bf16[256,320]{1,0:T(8,128)(2,1)} %bitcast.7, bf16[512,320]{1,0:T(8,128)(2,1)} %bitcast.5, ...), custom_call_target="tpu_custom_call" | custom-call | tf_op jit(solution)/shard_map/pallas_call | solution.py:403
  73.4 0.0 copy-start
  73.4 1.7 %copy.24 = bf16[16,16,320]{2,1,0:T(8,128)(2,1)} copy(bf16[16,16,320]{2,1,0:T(8,128)(2,1)} %bitcast.6) | data formatting | bytes 327680
  75.1 0.0 copy-done
  75.1 0.7 copy.25
Async XLA Ops:
  0.6 0.7 copy-start.1
  73.4 1.7 %copy-start = (bf16[512,320]{1,0:T(8,128)(2,1)S(1)}, bf16[512,320]{1,0:T(8,128)(2,1)}, u32[]{:S(2)}) copy-start(bf16[512,320]{1,0:T(8,128)(2,1)} %get-tuple-element.5) | copy-start | bytes 983044
